TPU v7x, 32 devices: a whole 2x2x4 slice. The times are simulated.
32 devices in a mesh: seq: 8 (over y, x, core), head: 4 (over z).
Axes of the slice: x: 2, y: 2, z: 4, core: 2. Of those that a mesh axis runs over, the one named last changes fastest.
Arguments:
- query_state: bfloat16 [12288, 512], P('seq'), may hold values from -6 to 6
- content: bfloat16 [12288, 512], P('seq'), may hold values from -6 to 6
- encoded: bfloat16 [12288, 512], P('seq'), may hold values from -6 to 6
- sentence_lengths: int32 [217], replicated, may hold values from 4 to 1024, as said below
- key_score: int32 [12288], replicated, may hold values from 0 to 63
- query_cut: int32 [12288], replicated, may hold values from 1 to 64
- w_query: bfloat16 [512, 512], P(None, 'head'), may hold values from -0.625 to 0.625
- w_key: bfloat16 [512, 512], P(None, 'head'), may hold values from -0.25 to 0.25
- w_value: bfloat16 [512, 512], P(None, 'head'), may hold values from -0.25 to 0.25
- w_out: bfloat16 [512, 512], P('head'), may hold values from -1.5 to 1.5
- gain_self: float32 [512], replicated, may hold values from 0.5 to 1.5
- w_cross_query: bfloat16 [512, 512], P(None, 'head'), may hold values from -0.625 to 0.625
- w_cross_key: bfloat16 [512, 512], P(None, 'head'), may hold values from -0.25 to 0.25
- w_cross_value: bfloat16 [512, 512], P(None, 'head'), may hold values from -0.25 to 0.25
- w_cross_out: bfloat16 [512, 512], P('head'), may hold values from -1.5 to 1.5
- gain_cross: float32 [512], replicated, may hold values from 0.5 to 1.5
- w_inner: bfloat16 [512, 2048], P(None, 'head'), may hold values from -0.25 to 0.25
- w_outer: bfloat16 [2048, 512], P('head'), may hold values from -0.1875 to 0.1875
- gain_final: float32 [512], replicated, may hold values from 0.5 to 1.5
- out_grad: bfloat16 [12288, 512], P('seq'), may hold values from -6 to 6
Outputs:
- mixed: bfloat16 [12288, 512], P('seq')
- query_state_grad: float32 [12288, 512], P('seq')
- content_grad: float32 [12288, 512], P('seq')
- encoded_grad: float32 [12288, 512], P('seq')
- w_query_grad: float32 [512, 512], P(None, 'head')
- w_key_grad: float32 [512, 512], P(None, 'head')
- w_value_grad: float32 [512, 512], P(None, 'head')
- w_out_grad: float32 [512, 512], P('head')
- gain_self_grad: float32 [512], replicated
- w_cross_query_grad: float32 [512, 512], P(None, 'head')
- w_cross_key_grad: float32 [512, 512], P(None, 'head')
- w_cross_value_grad: float32 [512, 512], P(None, 'head')
- w_cross_out_grad: float32 [512, 512], P('head')
- gain_cross_grad: float32 [512], replicated
- w_inner_grad: float32 [512, 2048], P(None, 'head')
- w_outer_grad: float32 [2048, 512], P('head')
- gain_final_grad: float32 [512], replicated
Inputs may be any that keep to these rules, and one draw needn't show every extreme that they name: `sentence_lengths`: exactly 6 entries equal 1024 (the documents); every other entry is a sentence of 4 to 56 tokens, one of them exactly 4; the entries sum to 12288; the order is drawn from the seed.
All inputs are finite; a program needn't handle non-finite values.
Results may differ from a plain program's by a relative error of at most 0.029.
The roundings to bfloat16 on the way count: a program that leaves them out, or rounds other values in their place, can miss the bound.
Values may be sent and summed in bfloat16 or wider, within the bound.
A program may use at most 384 MiB of HBM per device.

v0:
```python
from functools import partial
import math

import jax
import jax.numpy as jnp
from jax import lax
from jax.experimental import pallas as pl
from jax.experimental.pallas import tpu as pltpu
from jax.sharding import PartitionSpec as P

HEADS = 8
HEAD_SIZE = 64
PAIR = 2 * HEAD_SIZE
PAIRS = HEADS // 2
DOC_LEN = 1024
CHUNK = 528
LANES = 128
IN_FLIGHT = 2
EPS = 1e-05
NEG_BIG = -1e30
LOG2E = 1.4426950408889634
SCALE = 1.0 / math.sqrt(HEAD_SIZE)
SCORE_SCALE = SCALE * LOG2E
CODES = 128
BF16 = jnp.bfloat16
F32 = jnp.float32
VMEM_LIMIT = 60 << 20


def dot_nn(left, right):
    return lax.dot_general(left, right, (((1,), (0,)), ((), ())), preferred_element_type=F32)


def dot_nt(left, right):
    return lax.dot_general(left, right, (((1,), (1,)), ((), ())), preferred_element_type=F32)


def dot_tn(left, right):
    return lax.dot_general(left, right, (((0,), (0,)), ((), ())), preferred_element_type=F32)


def chunk_range(bounds):
    start = bounds[0, 0] // 16 * 16
    return start, (bounds[0, 1] - start + CHUNK - 1) // CHUNK


def chunk_rows(start, c):
    return pl.ds(pl.multiple_of(start + c * CHUNK, 16), CHUNK)


class Window:
    def __init__(self, bounds, source, held, sems):
        self.bounds, self.source, self.held, self.sems = bounds, source, held, sems
        self.start, self.chunks = chunk_range(bounds)

    def copy(self, c):
        rows = chunk_rows(self.start, c)
        return pltpu.make_async_copy(self.source.at[rows], self.held.at[rows], self.sems.at[c])

    def fetch(self):
        def one(c, carry):
            self.copy(c).start()
            return carry

        lax.fori_loop(0, self.chunks, one, 0)

    def loops(self, count, step):
        bounds, start, chunks = self.bounds, self.start, self.chunks

        def loop(number, size, where):
            def one(i, carry):
                c, lane = where(i)
                self.copy(c).wait()
                step(c, pl.ds(lane, size) if isinstance(lane, int) else pl.ds(pl.multiple_of(lane, LANES), size))
                return carry

            lax.fori_loop(0, number, one, 0)

        if count != 3 * LANES:
            return loop(chunks, count, lambda i: (i, 0))
        thirds = [(bounds[0, k] - start) // CHUNK for k in (2, 3)] + [(bounds[0, k] - start + CHUNK - 1) // CHUNK for k in (4, 5)]
        edges = [chunks * 0]
        for edge in thirds:
            edges.append(jnp.clip(edge, edges[-1], chunks))
        edges.append(chunks)

        def two(first, second, second_lane):
            number = edges[first + 1] - edges[first]

            def where(i):
                early = i < number
                return jnp.where(early, edges[first] + i, edges[second] + i - number), jnp.where(early, 0, second_lane)

            return number + edges[second + 1] - edges[second], where

        loop(edges[3] - edges[2], count, lambda i: (edges[2] + i, 0))
        number, where = two(1, 3, LANES)
        loop(number, 2 * LANES, where)
        number, where = two(0, 4, 2 * LANES)
        loop(number, LANES, where)


def layer_norm(resid):
    mean_row = jnp.mean(resid, axis=1, keepdims=True)
    centred = resid - mean_row
    var_row = jnp.mean(centred * centred, axis=1, keepdims=True)
    scale_row = lax.rsqrt(var_row + EPS)
    return centred * scale_row, scale_row


def norm_back(grad, normed, scale_row, gain):
    gain_grad = jnp.sum(grad * normed, axis=0, keepdims=True)
    scaled = grad * gain
    centre = jnp.mean(scaled, axis=1, keepdims=True)
    along = jnp.mean(scaled * normed, axis=1, keepdims=True)
    return scale_row * (scaled - centre - normed * along), gain_grad


def spread_heads(source, target):
    target[...] = jnp.zeros_like(target)
    for h in range(HEADS):
        row = h * PAIR + (h % 2) * HEAD_SIZE
        target[row : row + HEAD_SIZE, :] = source[h * HEAD_SIZE : (h + 1) * HEAD_SIZE, :]


def pair_rows(source, p, target):
    rows = source.shape[0]
    both = source[:, p * PAIR : (p + 1) * PAIR]
    lane = lax.broadcasted_iota(jnp.int32, both.shape, 1)
    zero = jnp.zeros_like(both)
    target[p, 0:rows, :] = jnp.where(lane < HEAD_SIZE, both, zero)
    target[p, rows : 2 * rows, :] = jnp.where(lane < HEAD_SIZE, zero, both)


MESH = pl.DeviceIdType.MESH


class Copies:
    def __init__(self, send, recv, local):
        self.send, self.recv, self.local = send, recv, local
        self.remotes, self.locals = 0, 0

    def remote(self, source, target, seq, part):
        k = self.remotes
        self.remotes += 1
        return pltpu.make_async_remote_copy(
            src_ref=source, dst_ref=target, send_sem=self.send.at[k], recv_sem=self.recv.at[k],
            device_id=(seq, part), device_id_type=MESH,
        )

    def own(self, source, target):
        k = self.locals
        self.locals += 1
        return pltpu.make_async_copy(source, target, self.local.at[k])


def greet(seq, part, peers, slices):
    barrier = pltpu.get_barrier_semaphore()
    for d in range(1, peers):
        pl.semaphore_signal(barrier, inc=1, device_id=(lax.rem(seq + d, peers), part), device_id_type=MESH)
    for d in range(1, slices):
        pl.semaphore_signal(barrier, inc=1, device_id=(seq, lax.rem(part + d, slices)), device_id_type=MESH)
    pl.semaphore_wait(barrier, peers - 1 + slices - 1)


def halo_sizes(part, count, rows):
    return max(0, DOC_LEN - part * count), max(0, (part + 1) * count + DOC_LEN - rows)


def put_rows(whole, part, row, ref, flip):
    value = ref[...]
    if flip:
        value = value.astype(F32).T.astype(BF16)
    whole[part, row : row + value.shape[0], :] = value


def pad_rows(whole, part, row):
    if row < whole.shape[1]:
        whole[part, row:, :] = jnp.zeros((whole.shape[1] - row, whole.shape[2]), BF16)


def find_sentences(begin, count, total_rows, lengths, score, cut, code, low, high_self, high_cross, bounds, blocks_code):
    blocks, lanes = score.shape
    pos = lax.broadcasted_iota(jnp.int32, (blocks, lanes), 0) * lanes + lax.broadcasted_iota(jnp.int32, (blocks, lanes), 1)
    pos = pos + (begin - DOC_LEN)
    own_pos = lax.broadcasted_iota(jnp.int32, (1, count), 1) + begin
    zero = jnp.zeros((blocks, lanes), jnp.int32)
    last_pos = begin + count - 1

    def one(s, carry):
        start, sentence, first, own_sentence, first_row, last_row, thirds = carry
        size = lengths[0, s]
        end = start + size
        passed = pos >= end
        sentence = sentence + jnp.where(passed, 1, 0)
        first = first + jnp.where(passed, size, 0)
        own_sentence = own_sentence + jnp.where(own_pos >= end, 1, 0)
        first_row = first_row + jnp.where(begin >= end, size, 0)
        last_row = last_row + jnp.where(last_pos >= start, size, 0)
        thirds = tuple(t + jnp.where(begin + LANES * (1 + k) >= end, size, 0) for k, t in enumerate(thirds[:2])) + tuple(
            t + jnp.where(begin + LANES * (1 + k) - 1 >= start, size, 0) for k, t in enumerate(thirds[2:])
        )
        return end, sentence, first, own_sentence, first_row, last_row, thirds

    none = lengths[0, 0] * 0
    carry = (none, zero, zero, jnp.zeros((1, count), jnp.int32), none, none, (none,) * 4)
    _, sentence, first, own_sentence, first_row, last_row, thirds = lax.fori_loop(0, lengths.shape[1], one, carry)
    shown = jnp.where(pos == first, -1, score[...])
    inside = jnp.logical_and(pos >= 0, pos < total_rows)
    blocks_code[0:blocks, :] = jnp.where(inside, sentence * CODES + shown, -CODES).astype(F32)
    for b in range(0, blocks, 8):
        turned = blocks_code[b : b + 8, :].T
        for j in range(min(8, blocks - b)):
            code[(b + j) * lanes : (b + j + 1) * lanes, :] = turned[:, j : j + 1]
    low[...] = (own_sentence * CODES - 1).astype(F32)
    high_self[...] = (own_sentence * CODES + cut[...]).astype(F32)
    high_cross[...] = (own_sentence * CODES + CODES // 2).astype(F32)
    origin = begin - DOC_LEN
    bounds[0, 0] = first_row - origin
    bounds[0, 1] = last_row - origin
    for k, row in enumerate(thirds):
        bounds[0, 2 + k] = row - origin


def start_kernel(
    peers, slices, count, content, encoded, query_state, out_grad, w_query, w_key, w_value, w_out,
    w_cross_query, w_cross_key, w_cross_value, w_cross_out, lengths, score, cut,
    content_window, encoded_window, all_one, all_two, own, own_out_grad, code, low, high_self, high_cross, bounds,
    send, recv, local, zeros, blocks_code,
):
    seq, part = lax.axis_index("seq"), lax.axis_index("head")
    chip, core = seq // 2, lax.rem(seq, 2)
    chips = peers // 2
    sibling = chip * 2 + 1 - core
    rows = content.shape[0]
    span = count + 2 * DOC_LEN
    spare = content_window.shape[0] - span
    copies = Copies(send, recv, local)
    cols = w_query.shape[1]
    for k, (ref, flip) in enumerate(((w_query, True), (w_key, True), (w_value, True))):
        put_rows(all_one, part, k * cols, ref, flip)
    pad_rows(all_one, part, 3 * cols)
    greet(seq, part, peers, slices)
    waits = []
    for source, target in ((query_state, own), (out_grad, own_out_grad)):
        mine = copies.own(source.at[pl.ds(pl.multiple_of(part * count, 16), count)], target)
        mine.start()
        waits.append(mine.wait)

    def halo(source, window):
        for k in range(slices):
            below, above = halo_sizes(k, count, rows)
            low = max(0, k * count - DOC_LEN)
            inner = span - below - above
            mine = copies.own(source.at[pl.ds(low, inner)], window.at[pl.ds(below, inner)])
            tail = copies.own(zeros.at[pl.ds(0, spare)], window.at[pl.ds(span, spare)])
            up = down = fill_low = fill_high = None
            if below:
                up = copies.remote(source.at[pl.ds(rows - below, below)], window.at[pl.ds(0, below)], seq + 1, part)
                fill_low = copies.own(zeros.at[pl.ds(0, below)], window.at[pl.ds(0, below)])
            if above:
                down = copies.remote(source.at[pl.ds(0, above)], window.at[pl.ds(span - above, above)], seq - 1, part)
                fill_high = copies.own(zeros.at[pl.ds(0, above)], window.at[pl.ds(span - above, above)])
            here, first, last = part == k, seq == 0, seq == peers - 1

            def start(mine=mine, tail=tail, up=up, down=down, fill_low=fill_low, fill_high=fill_high, here=here):
                @pl.when(here)
                def _():
                    if up is not None:
                        pl.when(jnp.logical_not(last))(up.start)
                        pl.when(first)(fill_low.start)
                    if down is not None:
                        pl.when(jnp.logical_not(first))(down.start)
                        pl.when(last)(fill_high.start)
                    mine.start()
                    tail.start()

            def finish(mine=mine, tail=tail, up=up, down=down, fill_low=fill_low, fill_high=fill_high, here=here):
                @pl.when(here)
                def _():
                    if up is not None:
                        pl.when(jnp.logical_not(last))(up.wait_send)
                        pl.when(jnp.logical_not(first))(up.wait_recv)
                        pl.when(first)(fill_low.wait)
                    if down is not None:
                        pl.when(jnp.logical_not(first))(down.wait_send)
                        pl.when(jnp.logical_not(last))(down.wait_recv)
                        pl.when(last)(fill_high.wait)
                    mine.wait()
                    tail.wait()

            start()
            waits.append(finish)

    packs = (all_one, all_two)

    def piece(ref, owner, index, size):
        return ref.at[owner, pl.ds(pl.multiple_of(index * size, 16), size)]

    across = {}
    for n, whole in enumerate(packs):
        size = whole.shape[1] // peers
        for d in range(1, slices):
            to = lax.rem(part + d, slices)
            across[n, d] = copies.remote(piece(whole, part, seq, size), piece(whole, part, seq, size), seq, to)
            across[n, d].start()
        if n == 0:
            zeros[...] = jnp.zeros_like(zeros)
            halo(content, content_window)
            put_rows(all_two, part, 0, w_out, False)
            for k, ref in enumerate((w_cross_query, w_cross_key, w_cross_value)):
                put_rows(all_two, part, (1 + k) * cols, ref, True)
            put_rows(all_two, part, 4 * cols, w_cross_out, False)
            pad_rows(all_two, part, 5 * cols)
    find_sentences(seq * rows + part * count, count, peers * rows, lengths, score, cut, code, low, high_self, high_cross, bounds, blocks_code)
    round_plane, to_sibling = {}, {}
    for n, whole in enumerate(packs):
        size = whole.shape[1] // peers
        for d in range(1, slices):
            across[n, d].wait_recv()
            owner = lax.rem(part + slices - d, slices)
            got = piece(whole, owner, seq, size)
            for e in range(1, chips):
                round_plane[n, d, e] = copies.remote(got, got, lax.rem(chip + e, chips) * 2 + core, part)
                round_plane[n, d, e].start()
            to_sibling[n, d, 0] = copies.remote(got, got, sibling, part)
            to_sibling[n, d, 0].start()
    halo(encoded, encoded_window)
    for n, whole in enumerate(packs):
        size = whole.shape[1] // peers
        for d in range(1, slices):
            owner = lax.rem(part + slices - d, slices)
            for e in range(1, chips):
                round_plane[n, d, e].wait_recv()
                got = piece(whole, owner, lax.rem(chip + chips - e, chips) * 2 + core, size)
                to_sibling[n, d, e] = copies.remote(got, got, sibling, part)
                to_sibling[n, d, e].start()
    for copy in to_sibling.values():
        copy.wait_recv()
    for copy in (*across.values(), *round_plane.values(), *to_sibling.values()):
        copy.wait_send()
    for wait in waits:
        wait()


def add_rows(target, source, target_at, source_at, size):
    step = 64 if size % 64 == 0 else 16

    def one(i, carry):
        to = pl.ds(pl.multiple_of(target_at + i * step, 16), step)
        by = pl.ds(pl.multiple_of(source_at + i * step, 16), step)
        target[to, :] = (target[to, :].astype(F32) + source[by, :].astype(F32)).astype(BF16)
        return carry

    lax.fori_loop(0, size // step, one, 0)


def end_kernel(
    peers, slices, count, blocks, parts, packs, plane_sums, outs, part_outs, pack_outs, scratch,
):
    seq, part = lax.axis_index("seq"), lax.axis_index("head")
    chip, core = seq // 2, lax.rem(seq, 2)
    chips = peers // 2
    sibling = chip * 2 + 1 - core
    rows = slices * count
    span = count + 2 * DOC_LEN
    send, recv, local = scratch[:3]
    copies = Copies(send, recv, local)
    first, last = seq == 0, seq == peers - 1
    start_line, end_line = part == 0, part == slices - 1
    greet(seq, part, peers, slices)
    sent = []

    def block(ref, index):
        return ref.at[pl.ds(pl.multiple_of(index * count, 16), count)]

    weight_scratch = scratch[3 : 3 + 3 * len(packs)]
    to_core, held = [], []
    for n, pack in enumerate(packs):
        half = pack.shape[1] // 2
        sibling_sum, mine = weight_scratch[3 * n : 3 * n + 2]
        copy = copies.remote(pack.at[:, pl.ds(pl.multiple_of((1 - core) * half, 16), half)], sibling_sum, sibling, part)
        copy.start()
        to_core.append(copy)
        keep = copies.own(pack.at[:, pl.ds(pl.multiple_of(core * half, 16), half)], mine)
        keep.start()
        held.append(keep)
        sent.append(copy)

    part_scratch = scratch[3 + 3 * len(packs) :]
    halos = []
    for n, grad in enumerate(parts):
        total, from_above, from_below = part_scratch[5 * n : 5 * n + 3]
        for k in range(slices):
            below, above = halo_sizes(k, count, rows)
            low = max(0, k * count - DOC_LEN)
            inner = span - below - above
            mine = copies.own(grad.at[pl.ds(below, inner)], total.at[pl.ds(low, inner)])
            down = up = None
            if below:
                down = copies.remote(grad.at[pl.ds(0, below)], from_above.at[pl.ds(0, below)], seq - 1, part)
            if above:
                up = copies.remote(grad.at[pl.ds(span - above, above)], from_below.at[pl.ds(0, above)], seq + 1, part)
            halos.append((n, k, below, above, low, inner, mine, down, up))

            @pl.when(part == k)
            def _(low=low, inner=inner, mine=mine, down=down, up=up, total=total):
                if down is not None:
                    pl.when(jnp.logical_not(first))(down.start)
                if up is not None:
                    pl.when(jnp.logical_not(last))(up.start)
                mine.start()
                if low:
                    total[0:low, :] = jnp.zeros((low, total.shape[1]), BF16)
                if low + inner < rows:
                    total[low + inner : rows, :] = jnp.zeros((rows - low - inner, total.shape[1]), BF16)

    def finish_halo(which):
        for n, k, below, above, low, inner, mine, down, up in halos:
            if n != which:
                continue
            total, from_above, from_below = part_scratch[5 * n : 5 * n + 3]

            @pl.when(part == k)
            def _(below=below, above=above, mine=mine, down=down, up=up, total=total, from_above=from_above, from_below=from_below):
                mine.wait()
                if down is not None:
                    pl.when(jnp.logical_not(first))(down.wait_send)

                    @pl.when(jnp.logical_not(last))
                    def _():
                        down.wait_recv()
                        add_rows(total, from_above, rows - below, 0, below)

                if up is not None:
                    pl.when(jnp.logical_not(last))(up.wait_send)

                    @pl.when(jnp.logical_not(first))
                    def _():
                        up.wait_recv()
                        add_rows(total, from_below, 0, 0, above)

    halves = 2 if slices <= 4 else 1
    sub = count // halves

    def unit_rows(ref, index, h, size=count, sub=sub):
        return ref.at[pl.ds(index * size + h * sub, sub)]

    def gather_rounds(out, me):
        rounds, flows = {}, ((1, slices - 1 - me), (-1, me))
        for sign, onward in flows:
            behind = me if sign > 0 else slices - 1 - me
            sends, waits = {}, {}
            for k in range(behind + 1):
                for h in range(halves):
                    ref = (me - sign * k, h)
                    if onward:
                        sends[k * halves + h] = ref
                    if k:
                        waits[k * halves + h] = ref
            rounds[sign] = (sends, waits)
        return rounds

    def line_gather(out, me, sems):
        steps, ends = [], []
        ring = gather_rounds(out, me)

        def onward(sign, i):
            ref = unit_rows(out, *ring[sign][0][i])
            return sems(sign, i, ref, ref, sign)

        def step(i):
            for sign in (1, -1):
                sends, waits = ring[sign]
                if i in waits:
                    sems(sign, i - halves, unit_rows(out, *waits[i]), unit_rows(out, *waits[i]), 0).wait_recv()
                if i in sends:
                    if i >= IN_FLIGHT:
                        onward(sign, i - IN_FLIGHT).wait_send()
                    onward(sign, i).start()

        def finish():
            for sign in (1, -1):
                sends, _ = ring[sign]
                for i in sorted(sends)[-IN_FLIGHT:]:
                    onward(sign, i).wait_send()

        return [partial(step, i) for i in range(slices * halves)], finish

    def line_sum(total, ins, out, me, sems, size=count, halves=halves):
        units, sub = (slices - 1) * halves, size // halves
        before = {1: [], -1: []}

        def place(sign, i):
            return slices - 1 - i // halves if sign > 0 else i // halves

        def slot(sign, i):
            return ins[0 if sign > 0 else 1].at[i]

        def onward(sign, i):
            return sems(sign, i, unit_rows(total, place(sign, i), i % halves, size, sub), slot(sign, i), sign)

        def step(r):
            for sign in (1, -1):
                depth = me if sign > 0 else slices - 1 - me
                i = r - depth
                if not 0 <= i < units:
                    continue
                b = place(sign, i)
                passes = b > me if sign > 0 else b < me
                if (passes or b == me) and depth:
                    sems(sign, i, slot(sign, i), slot(sign, i), 0).wait_recv()
                    add_rows(total, slot(sign, i), b * size + (i % halves) * sub, 0, sub)
                if passes:
                    if len(before[sign]) == IN_FLIGHT:
                        onward(sign, before[sign].pop(0)).wait_send()
                    before[sign].append(i)
                    onward(sign, i).start()

        def finish():
            for sign in (1, -1):
                for i in before[sign]:
                    onward(sign, i).wait_send()

        def place_own():
            if out is not None:
                out[pl.ds(me * size, size), :] = total[pl.ds(me * size, size), :]

        return [partial(step, r) for r in range(units + slices - 1)], place_own, finish

    def semaphores(units):
        base = copies.remotes
        copies.remotes += 2 * units

        def make(sign, i, source, target, to):
            k = base + i + (0 if sign > 0 else units)
            return pltpu.make_async_remote_copy(
                src_ref=source, dst_ref=target, send_sem=send.at[k], recv_sem=recv.at[k],
                device_id=(seq, part + to), device_id_type=MESH,
            )

        return make

    def interleave(*lists):
        for k in range(max((len(steps) for steps in lists), default=0)):
            for steps in lists:
                if k < len(steps):
                    steps[k]()

    def at_place(run):
        for me in range(slices):
            pl.when(part == me)(partial(run, me))

    own_copies = []
    for own, out in zip(blocks, outs):
        mine = copies.own(own, block(out, part))
        mine.start()
        own_copies.append(mine)
    plane_total, *plane_ins = part_scratch[5 * len(parts) :]
    pieces = [out.shape[0] // peers for out in pack_outs]
    piece_rows = sum(pieces)
    plane_sems = semaphores(slices)
    block_sems = [semaphores(slices * halves) for _ in outs]
    sum_sems = [semaphores(slices * halves) for _ in part_outs]
    after_sems = [semaphores(slices * halves) for _ in part_outs]

    to_chips = []

    def to_plane():
        for n, pack in enumerate(packs):
            half = pack.shape[1] // 2
            size = half // chips
            sibling_sum, mine, by_chip = weight_scratch[3 * n : 3 * n + 3]
            held[n].wait()
            to_core[n].wait_recv()

            def add_half(z, carry, sibling_sum=sibling_sum, mine=mine, half=half):
                add_rows(mine.at[z], sibling_sum.at[z], 0, 0, half)
                return carry

            lax.fori_loop(0, slices, add_half, 0)
            for e in range(1, chips):
                to = lax.rem(chip + e, chips)
                copy = copies.remote(mine.at[:, pl.ds(pl.multiple_of(to * size, 16), size)], by_chip.at[e - 1], to * 2 + core, part)
                copy.start()
                to_chips.append((n, e, copy))
                sent.append(copy)

    length = slices * halves
    plans = []
    for me in range(slices):
        gathers = [line_gather(out, me, sems) for out, sems in zip(outs, block_sems)]
        sums, afters = [], []
        for n, out in enumerate(part_outs):
            total, _, _, right_in, left_in = part_scratch[5 * n : 5 * n + 5]
            sums.append(line_sum(total, (right_in, left_in), out, me, sum_sems[n]))
            afters.append(line_gather(out, me, after_sems[n]))
        owned = [line_sum(plane_total, plane_ins, None, me, plane_sems, piece_rows, 1)]
        plans.append((gathers, sums, afters, owned))

    def rounds(me, *which):
        lists, ends = [], []
        for kind, n, low, high in which:
            entry = plans[me][kind][n]
            steps = entry[0]
            lists.append(steps[low:high])
            if low < len(steps) <= high:
                ends += list(entry[1:])
        interleave(*lists)
        for finish in ends:
            finish()

    def run(*which):
        at_place(lambda me: rounds(me, *which))

    def to_owners():
        for n, pack in enumerate(packs):
            half = pack.shape[1] // 2
            size, first_row = half // chips, sum(pieces[:n])
            mine, by_chip = weight_scratch[3 * n + 1 : 3 * n + 3]
            for m, e, copy in to_chips:
                if m == n:
                    copy.wait_recv()

            def add_plane(i, carry, mine=mine, by_chip=by_chip, size=size, first_row=first_row):
                z, r = i // (size // 16), lax.rem(i, size // 16)
                at = pl.ds(pl.multiple_of(r * 16, 16), 16)
                value = mine[z, pl.ds(pl.multiple_of(chip * size + r * 16, 16), 16), :].astype(F32)
                for e in range(chips - 1):
                    value = value + by_chip[e, z, at, :].astype(F32)
                plane_total[pl.ds(pl.multiple_of(z * piece_rows + first_row + r * 16, 16), 16), :] = value.astype(BF16)
                return carry

            lax.fori_loop(0, slices * (size // 16), add_plane, 0)

    def piece_at(n, of_chip, of_core):
        size = pack_outs[n].shape[0] // peers
        index = of_core * chips + of_chip if n < len(packs) else of_chip * 2 + of_core
        return pl.multiple_of(index * size, 16), size

    round_plane, to_sibling = [], []

    def back_to_plane():
        for n, out in enumerate(pack_outs):
            start, size = piece_at(n, chip, core)

            def keep(r, carry, out=out, start=start, first_row=sum(pieces[:n])):
                at = pl.ds(pl.multiple_of(part * piece_rows + first_row + r * 16, 16), 16)
                out[pl.ds(pl.multiple_of(start + r * 16, 16), 16), :] = plane_total[at, :]
                return carry

            lax.fori_loop(0, size // 16, keep, 0)
            piece = out.at[pl.ds(start, size)]
            for e in range(1, chips):
                copy = copies.remote(piece, piece, lax.rem(chip + e, chips) * 2 + core, part)
                copy.start()
                round_plane.append((n, e, copy))
                sent.append(copy)
            copy = copies.remote(piece, piece, sibling, part)
            copy.start()
            round_plane.append((n, 0, copy))
            sent.append(copy)

    sum_length = (slices - 1) * halves + slices - 1
    plane_copies = []
    for n, summed in enumerate(plane_sums):
        first_row, size = sum(pieces[: len(packs) + n]), pieces[len(packs) + n]
        for z in range(slices):
            plane_copies.append(copies.own(summed.at[z], plane_total.at[pl.ds(z * piece_rows + first_row, size)]))
    for keep in plane_copies:
        keep.start()
    for mine in own_copies:
        mine.wait()
    run((0, 0, 0, 2))
    to_plane()
    run((0, 0, 2, 3))
    finish_halo(0)
    run((0, 0, 3, length), (1, 0, 0, sum_length))
    for keep in plane_copies:
        keep.wait()
    if len(parts) > 1:
        finish_halo(1)
        run((1, 1, 0, sum_length // 2), (2, 0, 0, sum_length // 2))
        to_owners()
        run((1, 1, sum_length // 2, sum_length), (2, 0, sum_length // 2, length))
    else:
        to_owners()
    last = len(parts) - 1
    run((3, 0, 0, 2 * (slices - 1)), (2, last, 0, length // 2))
    back_to_plane()
    run((2, last, length // 2, length))
    for n, e, copy in round_plane:
        copy.wait_recv()
        if e:
            start, size = piece_at(n, lax.rem(chip + chips - e, chips), core)
            piece = pack_outs[n].at[pl.ds(start, size)]
            copy = copies.remote(piece, piece, sibling, part)
            copy.start()
            to_sibling.append(copy)
            sent.append(copy)
    for copy in to_sibling:
        copy.wait_recv()
    for copy in sent:
        copy.wait_send()


class Rows:
    def __init__(self, pack, index, size):
        self.pack, self.at = pack, slice(index * size, (index + 1) * size)

    def __getitem__(self, _):
        value = self.pack[:, self.at, :]
        return value.reshape(value.shape[0] * value.shape[1], value.shape[2])


def write_rows(pack, index, size, value):
    slices = pack.shape[0]
    pack[:, index * size : (index + 1) * size, :] = value.astype(BF16).reshape(slices, size, value.shape[1])


def write_pieces(pack, z, row, value):
    size = pack.shape[2]
    for i in range(value.shape[0] // size):
        pack[row // size + i, z] = value[i * size : (i + 1) * size, :].astype(BF16)


def mask_bias(code, low, high):
    return jnp.where((code >= low) & (code < high), 0.0, NEG_BIG).astype(F32)


def pair_product(left, spread, p, see):
    count = see.size
    blocks = [spread[h * PAIR : (h + 1) * PAIR, see] for h in (2 * p, 2 * p + 1)]
    if count % LANES:
        return [dot_nn(left, block) for block in blocks]
    both = dot_nn(left, jnp.concatenate(blocks, axis=1))
    return both[:, :count], both[:, count:]


def attend(window, code, low, high, w_key_t, w_value_t, spread, bias, top, total, out):
    top[...] = jnp.full_like(top, NEG_BIG)
    total[...] = jnp.zeros_like(total)
    out[...] = jnp.zeros_like(out)

    def step(c, see):
        at = chunk_rows(window.start, c)
        rows = window.held[at, :]
        keys = dot_nt(rows, w_key_t[...]).astype(BF16)
        values_t = dot_nt(rows, w_value_t[...]).astype(BF16).T
        bias[:, see] = mask_bias(code[at, :], low[:, see], high[:, see])
        for h in range(HEADS):
            p = h // 2
            if h % 2 == 0:
                both = pair_product(keys[:, p * PAIR : (p + 1) * PAIR], spread, p, see)
            scores = both[h % 2] * SCORE_SCALE + bias[:, see]
            before = top[h : h + 1, see]
            now = jnp.maximum(before, jnp.max(scores, axis=0, keepdims=True))
            weights = jnp.exp2(scores - now)
            shrink = jnp.exp2(before - now)
            top[h : h + 1, see] = now
            total[h : h + 1, see] = total[h : h + 1, see] * shrink + jnp.sum(weights, axis=0, keepdims=True)
            head = slice(h * HEAD_SIZE, (h + 1) * HEAD_SIZE)
            out[head, see] = out[head, see] * shrink + dot_nn(values_t[head, :], weights.astype(BF16))

    window.loops(out.shape[1], step)
    for h in range(HEADS):
        head = slice(h * HEAD_SIZE, (h + 1) * HEAD_SIZE)
        out[head, :] = out[head, :] / total[h : h + 1, :]


def attend_back(
    window, code, low, high, w_key_t, w_value_t, spread, grad_spread, pairs, grad_pairs, lse, delta, bias,
    query_grad, window_grad, w_key_grad, w_value_grad,
):
    count = spread.shape[1]
    query_grad[...] = jnp.zeros_like(query_grad)
    w_key_grad[...] = jnp.zeros_like(w_key_grad)
    w_value_grad[...] = jnp.zeros_like(w_value_grad)
    window_grad[...] = jnp.zeros_like(window_grad)

    def step(c, see):
        at = chunk_rows(window.start, c)
        seen = (see, pl.ds(count + see.start, see.size) if isinstance(see.start, int) else pl.ds(pl.multiple_of(count + see.start, LANES), see.size))
        rows = window.held[at, :]
        keys = dot_nt(rows, w_key_t[...]).astype(BF16)
        keys_t = keys.T
        values = dot_nt(rows, w_value_t[...]).astype(BF16)
        bias[:, see] = mask_bias(code[at, :], low[:, see], high[:, see])
        key_grads, value_grads = [], []
        for p in range(PAIRS):
            columns = slice(p * PAIR, (p + 1) * PAIR)
            probs, score_grads = [], []
            both_scores = pair_product(keys[:, columns], spread, p, see)
            both_dprobs = pair_product(values[:, columns], grad_spread, p, see)
            for h in (2 * p, 2 * p + 1):
                head = slice(h * HEAD_SIZE, (h + 1) * HEAD_SIZE)
                prob = jnp.exp2(both_scores[h % 2] * SCORE_SCALE + bias[:, see] - lse[h : h + 1, see])
                score_grad = (prob * (both_dprobs[h % 2] - delta[h : h + 1, see])).astype(BF16)
                query_grad[head, see] += dot_nn(keys_t[head, :], score_grad)
                probs.append(prob.astype(BF16))
                score_grads.append(score_grad)
            if count % LANES == 0:
                both = jnp.concatenate([pairs[p, r, :] for r in seen], axis=0)
                grad_both = jnp.concatenate([grad_pairs[p, r, :] for r in seen], axis=0)
                key_grads.append(dot_nn(jnp.concatenate(score_grads, axis=1), both))
                value_grads.append(dot_nn(jnp.concatenate(probs, axis=1), grad_both))
            else:
                key_grads.append(sum(dot_nn(x, pairs[p, r, :]) for x, r in zip(score_grads, seen)))
                value_grads.append(sum(dot_nn(x, grad_pairs[p, r, :]) for x, r in zip(probs, seen)))
        keys_low = (jnp.concatenate(key_grads, axis=1) * SCALE).astype(BF16)
        values_low = jnp.concatenate(value_grads, axis=1).astype(BF16)
        window_grad[at, :] = (dot_nn(keys_low, w_key_t[...]) + dot_nn(values_low, w_value_t[...])).astype(window_grad.dtype)
        w_key_grad[...] += dot_tn(rows, keys_low)
        w_value_grad[...] += dot_tn(rows, values_low)

    window.loops(count, step)


def forward_kernel(
    cols, bounds, own, content_window, encoded_window, gain, code, low, high_self, high_cross, pack_one, pack_two_in,
    self_t, lse_self, hidden, cross_t, lse_cross,
    spread, bias, top, total, low_t, content_held, encoded_held, pack_two, content_sems, encoded_sems, pack_sem,
):
    content = Window(bounds, content_window, content_held, content_sems)
    encoded = Window(bounds, encoded_window, encoded_held, encoded_sems)
    content.fetch()
    whole_pack = pltpu.make_async_copy(pack_two_in, pack_two, pack_sem.at[0])
    whole_pack.start()
    encoded.fetch()
    w_query_t, w_key_t, w_value_t = (Rows(pack_one, k, cols) for k in range(3))
    low_t[...] = dot_nt(w_query_t[...], own[...]).astype(BF16)
    spread_heads(low_t, spread)
    attend(content, code, low, high_self, w_key_t, w_value_t, spread, bias, top, total, self_t)
    lse_self[...] = top[...] + jnp.log2(total[...])
    whole_pack.wait()
    w_out, w_query_t, w_key_t, w_value_t = (Rows(pack_two, k, cols) for k in range(4))
    branch = dot_tn(self_t[...].astype(BF16), w_out[...])
    normed, _ = layer_norm(own[...].astype(F32) + branch)
    hidden[...] = normed * gain[...]
    low_t[...] = dot_nt(w_query_t[...], hidden[...].astype(BF16)).astype(BF16)
    spread_heads(low_t, spread)
    attend(encoded, code, low, high_cross, w_key_t, w_value_t, spread, bias, top, total, cross_t)
    lse_cross[...] = top[...] + jnp.log2(total[...])


def ffn_kernel(
    cols, hidden_one, cross_t, pack_two, gain_cross, pack_three_in, gain_final, out_grad,
    mixed, resid_grad, w_out_grad, grad_three_out, gain_cross_grad, gain_final_grad,
    normed_two, hidden_two_low, slope, active, sum_ffn, pack_out, pack_three, grad_three_pack, sems, out_sems,
):
    slices, units = pack_three.shape[0], pack_three.shape[1] // 2
    out_copy = pltpu.make_async_copy(pack_two.at[:, pl.ds(4 * cols, cols)], pack_out, sems.at[slices])
    out_copy.start()
    slice_copies = [pltpu.make_async_copy(pack_three_in.at[z], pack_three.at[z], sems.at[z]) for z in range(slices)]
    for copy in slice_copies:
        copy.start()
    out_copy.wait()
    w_out = Rows(pack_out, 0, cols)
    cross_low = cross_t[...].astype(BF16)
    normed, scale_two = layer_norm(hidden_one[...] + dot_tn(cross_low, w_out[...]))
    normed_two[...] = normed
    hidden_two = normed * gain_cross[...]
    hidden_two_low[...] = hidden_two.astype(BF16)
    sum_ffn[...] = hidden_two
    for z in range(slices):
        slice_copies[z].wait()
        inner = dot_nt(hidden_two_low[...], pack_three[z, 0:units, :])
        below = 0.5 * (1.0 + lax.erf(inner * math.sqrt(0.5)))
        slope[z] = below + inner * (jnp.exp2(inner * inner * (-0.5 * LOG2E)) * (1.0 / math.sqrt(2.0 * math.pi)))
        active[z] = (inner * below).astype(BF16)
        sum_ffn[...] += dot_nn(active[z], pack_three[z, units:, :])
    normed_three, scale_three = layer_norm(sum_ffn[...])
    mixed[...] = (normed_three * gain_final[...]).astype(BF16)
    grad_three, gain_grad = norm_back(out_grad[...].astype(F32), normed_three, scale_three, gain_final[...])
    gain_final_grad[...] = gain_grad
    ffn_low = grad_three.astype(BF16)
    result_copies = [pltpu.make_async_copy(grad_three_pack.at[:, z], grad_three_out.at[:, z], out_sems.at[z]) for z in range(slices)]
    sum_ffn[...] = grad_three
    for z in range(slices):
        write_pieces(grad_three_pack, z, units, dot_tn(active[z], ffn_low))
        inner_low = (dot_nt(ffn_low, pack_three[z, units:, :]) * slope[z]).astype(BF16)
        write_pieces(grad_three_pack, z, 0, dot_tn(inner_low, hidden_two_low[...]))
        sum_ffn[...] += dot_nn(inner_low, pack_three[z, 0:units, :])
        result_copies[z].start()
    grad, gain_grad = norm_back(sum_ffn[...], normed_two[...], scale_two, gain_cross[...])
    gain_cross_grad[...] = gain_grad
    resid_grad[...] = grad
    w_out_grad[...] = dot_nn(cross_low, grad.astype(BF16)).astype(BF16)
    for copy in result_copies:
        copy.wait()


def prepare_back(query, query_t, grad, grad_t, out, spread, grad_spread, pairs, grad_pairs, delta, low_t):
    low_t[...] = query_t.astype(BF16)
    spread_heads(low_t, spread)
    for p in range(PAIRS):
        pair_rows(query.astype(BF16), p, pairs)
        pair_rows(grad.astype(BF16), p, grad_pairs)
    low_t[...] = grad_t.astype(BF16)
    spread_heads(low_t, grad_spread)
    for h in range(HEADS):
        head = slice(h * HEAD_SIZE, (h + 1) * HEAD_SIZE)
        delta[h : h + 1, :] = jnp.sum(low_t[head, :].astype(F32) * out[head, :], axis=0, keepdims=True)


def cross_back_kernel(
    cols, bounds, own, self_t, gain, resid_two_grad, cross_t, lse, window_in, code, low, high, pack_two,
    w_cross_out_grad, gain_cross_grad, gain_final_grad, resid_one_grad, window_out, grad_two_pack,
    spread, grad_spread, pairs, grad_pairs, delta, bias, low_t, query_grad, key_sum, value_sum, held, window_grad, sems, out_sem,
    normed_one, scale_one,
):
    window = Window(bounds, window_in, held, sems)
    window.fetch()
    w_out, w_query_t, w_key_t, w_value_t, w_cross_out = (Rows(pack_two, k, cols) for k in range(5))
    self_low = self_t[...].astype(BF16)
    normed, scale = layer_norm(own[...].astype(F32) + dot_tn(self_low, w_out[...]))
    normed_one[...] = normed
    scale_one[...] = scale
    hidden_low = (normed * gain[...]).astype(BF16)
    branch_low = resid_two_grad[...].astype(BF16)
    prepare_back(
        dot_nt(hidden_low, w_query_t[...]), dot_nt(w_query_t[...], hidden_low),
        dot_nt(branch_low, w_cross_out[...]), dot_nt(w_cross_out[...], branch_low),
        cross_t, spread, grad_spread, pairs, grad_pairs, delta, low_t,
    )
    attend_back(
        window, code, low, high, w_key_t, w_value_t, spread, grad_spread, pairs, grad_pairs, lse, delta, bias,
        query_grad, window_grad, key_sum, value_sum,
    )
    result = pltpu.make_async_copy(window_grad, window_out, out_sem.at[0])
    result.start()
    query_low = (query_grad[...] * SCALE).astype(BF16)
    hidden_low = (normed_one[...] * gain[...]).astype(BF16)
    grad_one = resid_two_grad[...] + dot_tn(query_low, w_query_t[...])
    grad, gain_sum = norm_back(grad_one, normed_one[...], scale_one[...], gain[...])
    resid_one_grad[...] = grad
    write_rows(grad_two_pack, 0, cols, dot_nn(self_t[...].astype(BF16), grad.astype(BF16)))
    write_rows(grad_two_pack, 1, cols, dot_nn(query_low, hidden_low))
    write_rows(grad_two_pack, 2, cols, key_sum[...].T)
    write_rows(grad_two_pack, 3, cols, value_sum[...].T)
    write_rows(grad_two_pack, 4, cols, w_cross_out_grad[...])
    slices, rows, width = grad_two_pack.shape
    gains = jnp.concatenate([gain_sum, gain_cross_grad[...], gain_final_grad[...], jnp.zeros((13, width), F32)], axis=0)
    for z in range(slices):
        grad_two_pack[z, 5 * cols : 5 * cols + 16, :] = gains.astype(BF16)
        if rows > 5 * cols + 16:
            grad_two_pack[z, 5 * cols + 16 :, :] = jnp.zeros((rows - 5 * cols - 16, width), BF16)
    result.wait()


def self_back_kernel(
    cols, bounds, own, resid_one_grad, pack_two, self_t, lse, window_in, code, low, high, pack_one,
    own_grad, window_out, grad_one_pack,
    spread, grad_spread, pairs, grad_pairs, delta, bias, low_t, query_grad, key_sum, value_sum, held, window_grad, sems, out_sem,
    pack_out, pack_sem,
):
    out_copy = pltpu.make_async_copy(pack_two.at[:, pl.ds(0, cols)], pack_out, pack_sem.at[0])
    out_copy.start()
    window = Window(bounds, window_in, held, sems)
    window.fetch()
    out_copy.wait()
    w_query_t, w_key_t, w_value_t = (Rows(pack_one, k, cols) for k in range(3))
    w_out = Rows(pack_out, 0, cols)
    branch_low = resid_one_grad[...].astype(BF16)
    prepare_back(
        dot_nt(own[...], w_query_t[...]), dot_nt(w_query_t[...], own[...]),
        dot_nt(branch_low, w_out[...]), dot_nt(w_out[...], branch_low),
        self_t, spread, grad_spread, pairs, grad_pairs, delta, low_t,
    )
    attend_back(
        window, code, low, high, w_key_t, w_value_t, spread, grad_spread, pairs, grad_pairs, lse, delta, bias,
        query_grad, window_grad, key_sum, value_sum,
    )
    result = pltpu.make_async_copy(window_grad, window_out, out_sem.at[0])
    result.start()
    query_low = (query_grad[...] * SCALE).astype(BF16)
    write_rows(grad_one_pack, 0, cols, dot_nn(query_low, own[...]))
    write_rows(grad_one_pack, 1, cols, key_sum[...].T)
    write_rows(grad_one_pack, 2, cols, value_sum[...].T)
    slices, rows, width = grad_one_pack.shape
    if rows > 3 * cols:
        grad_one_pack[:, 3 * cols :, :] = jnp.zeros((slices, rows - 3 * cols, width), BF16)
    own_grad[...] = (resid_one_grad[...] + dot_tn(query_low, w_query_t[...])).astype(BF16)
    result.wait()


def finish_kernel(cols, units, slices, part, *refs):
    blocks, rows_in, (sum_one, sum_two, sum_three) = refs[:slices], refs[slices : slices + 3], refs[slices + 3 : slices + 6]
    outs = refs[slices + 6 :]
    step = pl.program_id(0)
    came = lax.rem(part[0, 0] + slices - step, slices)
    for d, ref in enumerate(blocks):

        @pl.when(came == d)
        def _(ref=ref):
            outs[0][...] = ref[...]

    for source, target in zip(rows_in, outs[1:4]):
        target[...] = source[...].astype(F32)

    def weights(k):
        w_query, w_key, w_value, w_out, w_cross_query, w_cross_key, w_cross_value, w_cross_out, w_inner, w_outer = outs[4:14]
        width = sum_one.shape[1]
        wide, tall, unit_rows = width // slices, cols // slices, units // slices
        some = slice(k * wide, (k + 1) * wide)
        for n, target in enumerate((w_query, w_key, w_value)):
            target[...] = sum_one[n * cols : (n + 1) * cols, some].astype(F32).T
        for n, target in enumerate((w_cross_query, w_cross_key, w_cross_value)):
            target[...] = sum_two[(1 + n) * cols : (2 + n) * cols, some].astype(F32).T
        w_out[...] = sum_two[k * tall : (k + 1) * tall, :].astype(F32)
        w_cross_out[...] = sum_two[4 * cols + k * tall : 4 * cols + (k + 1) * tall, :].astype(F32)
        w_inner[...] = sum_three[0:units, some].astype(F32).T
        w_outer[...] = sum_three[units + k * unit_rows : units + (k + 1) * unit_rows, :].astype(F32)

    for k in range(slices):
        pl.when(step == k)(partial(weights, k))

    @pl.when(step == 0)
    def _():
        gains = sum_two[5 * cols : 5 * cols + 16, :].astype(F32)
        for k, target in enumerate(outs[14:17]):
            target[...] = gains[k : k + 1, :]


def call(kernel, outs, scratch, smem, *args, far=(), far_outs=(), micros=20):
    def space(k, left, scalars):
        return pl.ANY if k in left else pltpu.SMEM if k < scalars else pltpu.VMEM

    return pl.pallas_call(
        kernel,
        out_shape=[jax.ShapeDtypeStruct(shape, kind) for shape, kind in outs],
        in_specs=[pl.BlockSpec(memory_space=space(k, far, smem)) for k in range(len(args))],
        out_specs=[pl.BlockSpec(memory_space=space(k, far_outs, 0)) for k in range(len(outs))],
        scratch_shapes=[pltpu.SemaphoreType.DMA((shape,)) if kind is None else pltpu.VMEM(shape, kind) for shape, kind in scratch],
        compiler_params=pltpu.CompilerParams(vmem_limit_bytes=VMEM_LIMIT),
        cost_estimate=pl.CostEstimate(flops=micros * 10**9, bytes_accessed=micros * 10**6, transcendentals=0),
    )(*args)


def padded(size, unit):
    return -(-size // unit) * unit


def talk(kernel, outs, out_spaces, scratch, copies, number, spaces, *args):
    return pl.pallas_call(
        kernel,
        out_shape=[jax.ShapeDtypeStruct(shape, kind) for shape, kind in outs],
        in_specs=[pl.BlockSpec(memory_space=space) for space in spaces],
        out_specs=[pl.BlockSpec(memory_space=space) for space in out_spaces],
        scratch_shapes=[pltpu.SemaphoreType.DMA((n,)) for n in (copies[0], copies[0], copies[1])] + [pltpu.VMEM(shape, kind) for shape, kind in scratch],
        compiler_params=pltpu.CompilerParams(vmem_limit_bytes=VMEM_LIMIT, collective_id=number, has_side_effects=True),
        cost_estimate=pl.CostEstimate(flops=80 * 10**9, bytes_accessed=80 * 10**6, transcendentals=0),
    )(*args)


def body(
    query_state, content, encoded, sentence_lengths, key_score, query_cut, w_query, w_key, w_value, w_out, gain_self,
    w_cross_query, w_cross_key, w_cross_value, w_cross_out, gain_cross, w_inner, w_outer, gain_final, out_grad,
):
    rows, width = query_state.shape
    slices = lax.axis_size("head")
    count = rows // slices
    lanes = math.gcd(count, LANES)
    wide = padded(count + 2 * DOC_LEN + CHUNK, lanes)
    spare = wide - count - 2 * DOC_LEN
    seq, part = lax.axis_index("seq"), lax.axis_index("head")
    begin = seq * rows + part * count
    score = lax.dynamic_slice_in_dim(jnp.pad(key_score, (DOC_LEN, DOC_LEN + spare)), begin, wide, 0).reshape(wide // lanes, lanes)
    cut = lax.dynamic_slice_in_dim(query_cut, begin, count, 0).reshape(1, count)
    gain_self, gain_cross, gain_final = (g.reshape(1, width) for g in (gain_self, gain_cross, gain_final))

    peers = lax.axis_size("seq")
    chips = peers // 2
    cols, units = w_query.shape[1], w_inner.shape[1]
    unit = 16 * peers
    sizes = [padded(n, unit) for n in (3 * cols, 5 * cols, 2 * units)]
    grad_sizes = [sizes[0], padded(5 * cols + 16, unit), sizes[2]]

    share = sizes[2] // peers
    slice_three = jnp.concatenate([w_inner.T, w_outer, jnp.zeros((sizes[2] - 2 * units, width), BF16)], axis=0)
    share_three = lax.dynamic_slice_in_dim(slice_three, seq * share, share, 0)
    pack_three = lax.all_gather(share_three, ("head", "seq"), axis=0, tiled=True).reshape(slices, sizes[2], width)
    start_copies = 2 * (slices - 1) * (2 * chips) + 4 * slices
    hbm, vmem, smem = pl.ANY, pltpu.VMEM, pltpu.SMEM
    (
        content_window, encoded_window, pack_one, pack_two, own, own_out_grad, code, low, high_self, high_cross, bounds,
    ) = talk(
        partial(start_kernel, peers, slices, count),
        [((wide, width), BF16)] * 2 + [((slices, n, width), BF16) for n in sizes[:2]] + [((count, width), BF16)] * 2
        + [((wide, 1), F32)] + [((1, count), F32)] * 3 + [((1, 6), jnp.int32)],
        [vmem] * 10 + [smem],
        [((DOC_LEN, width), BF16), ((padded(wide // lanes, 8), lanes), F32)], (start_copies, 8 * slices + 16), 0,
        [hbm] * 4 + [vmem] * 8 + [smem] + [vmem] * 2,
        content, encoded, query_state, out_grad, w_query, w_key, w_value, w_out,
        w_cross_query, w_cross_key, w_cross_value, w_cross_out, sentence_lengths.reshape(1, -1), score, cut,
    )

    def split_refs(kernel, ins, outs):
        def run(*refs):
            return kernel(refs[:ins], refs[ins : ins + outs], refs[ins + outs :])
        return run

    touched = -(-wide // CHUNK)
    window_held = [((wide, width), BF16)]
    self_t, lse_self, hidden_one, cross_t, lse_cross = call(
        partial(forward_kernel, cols),
        [((width, count), F32), ((HEADS, count), F32), ((count, width), F32), ((width, count), F32), ((HEADS, count), F32)],
        [((HEADS * PAIR, count), BF16), ((CHUNK, count), F32), ((HEADS, count), F32), ((HEADS, count), F32), ((width, count), BF16)]
        + window_held * 2 + [((slices, sizes[1], width), BF16), (touched, None), (touched, None), (1, None)], 1,
        bounds, own, content_window, encoded_window, gain_self, code, low, high_self, high_cross, pack_one, pack_two, far=(2, 3, 10),
    )
    mixed, resid_two_grad, w_cross_out_grad, grads_three, gain_cross_grad, gain_final_grad = call(
        partial(ffn_kernel, cols),
        [
            ((count, width), BF16), ((count, width), F32), ((width, width), BF16), ((peers, slices, grad_sizes[2] // peers, width), BF16),
            ((1, width), F32), ((1, width), F32),
        ],
        [
            ((count, width), F32), ((count, width), BF16), ((slices, count, units), F32),
            ((slices, count, units), BF16), ((count, width), F32), ((slices, cols, width), BF16), ((slices, sizes[2], width), BF16),
            ((peers, slices, grad_sizes[2] // peers, width), BF16), (slices + 1, None), (slices, None),
        ], 0,
        hidden_one, cross_t, pack_two, gain_cross, pack_three, gain_final, own_out_grad, far=(2, 4), far_outs=(3,),
    )
    back = [
        ((HEADS * PAIR, count), BF16), ((HEADS * PAIR, count), BF16), ((PAIRS, 2 * count, PAIR), BF16),
        ((PAIRS, 2 * count, PAIR), BF16), ((HEADS, count), F32), ((CHUNK, count), F32), ((width, count), BF16),
        ((width, count), F32), ((width, width), F32), ((width, width), F32),
    ] + window_held * 2 + [(touched, None), (1, None)]
    resid_one_grad, encoded_part, grads_two = call(
        partial(cross_back_kernel, cols),
        [((count, width), F32), ((wide, width), BF16), ((slices, grad_sizes[1], width), BF16)],
        back + [((count, width), F32), ((count, 1), F32)], 1,
        bounds, own, self_t, gain_self, resid_two_grad, cross_t, lse_cross, encoded_window, code, low, high_cross, pack_two,
        w_cross_out_grad, gain_cross_grad, gain_final_grad, far=(7,), far_outs=(1,), micros=4,
    )
    own_grad, content_part, grads_one = call(
        partial(self_back_kernel, cols),
        [((count, width), BF16), ((wide, width), BF16), ((slices, grad_sizes[0], width), BF16)],
        back + [((slices, cols, width), BF16), (1, None)], 1,
        bounds, own, resid_one_grad, pack_two, self_t, lse_self, content_window, code, low, high_self, pack_one,
        far=(3, 6), far_outs=(1,), micros=4,
    )

    mixed_blocks = [mixed] + [lax.ppermute(mixed, "head", [(i, (i + d) % slices) for i in range(slices)]) for d in range(1, slices)]
    plane_three = lax.psum_scatter(grads_three, "seq", scatter_dimension=0, tiled=True).reshape(grads_three.shape[1:])
    blocks, parts, grads, planes = [own_grad], [content_part, encoded_part], [grads_one, grads_two], [plane_three]
    weight_scratch = []
    for n in grad_sizes[: len(grads)]:
        half, size = n // 2, n // 2 // chips
        weight_scratch += [
            ((slices, half, width), BF16), ((slices, half, width), BF16), ((chips - 1, slices, size, width), BF16),
        ]
    halves = 2 if slices <= 4 else 1
    units_in = (slices - 1) * halves
    part_scratch = [
        ((rows, width), BF16), ((DOC_LEN, width), BF16), ((DOC_LEN, width), BF16),
        ((units_in, count // halves, width), BF16), ((units_in, count // halves, width), BF16),
    ] * len(parts)
    piece_rows = sum(grad_sizes) // peers
    plane_scratch = [((slices * piece_rows, width), BF16)] + [((slices - 1, piece_rows, width), BF16)] * 2
    ins, outs = (len(blocks), len(parts), len(grads), len(planes)), (len(blocks), len(parts), len(grad_sizes))

    def end(refs, out_refs, scratch):
        a, b, c = ins[0], ins[0] + ins[1], sum(ins[:3])
        end_kernel(
            peers, slices, count, refs[:a], refs[a:b], refs[b:c], refs[c:], out_refs[: outs[0]],
            out_refs[outs[0] : outs[0] + outs[1]], out_refs[outs[0] + outs[1] :], scratch,
        )

    end_copies = len(grad_sizes) * (1 + 3 * (chips - 1) + slices) + 2 * slices + len(parts) * 2 * slices + (len(blocks) + 2 * len(parts)) * 2 * slices * halves
    results = talk(
        split_refs(end, sum(ins), sum(outs)),
        [((rows, width), BF16)] * (len(blocks) + len(parts)) + [((n, width), BF16) for n in grad_sizes], [vmem] * sum(outs),
        weight_scratch + part_scratch + plane_scratch, (end_copies, 8 * slices + 8), 1, [hbm] * sum(ins), *blocks, *parts, *grads, *planes,
    )
    query_state_grad, content_grad, encoded_grad, sum_one, sum_two, sum_three = results

    square, tall = ((width, cols), F32), ((cols, width), F32)
    finals = [((rows, width), BF16)] + [((rows, width), F32)] * 3 + [square] * 3 + [tall, square, square, square, tall]
    finals += [((width, units), F32), ((units, width), F32)] + [((1, width), F32)] * 3
    by_rows = pl.BlockSpec((count, width), lambda i: (i, 0))

    def whole(shape):
        return pl.BlockSpec(shape, lambda i: (0,) * len(shape))

    def by_step(shape):
        return pl.BlockSpec((shape[0] // slices, shape[1]), lambda i: (i, 0))

    sums = [sum_one, sum_two, sum_three]
    results = pl.pallas_call(
        partial(finish_kernel, cols, units, slices),
        grid=(slices,),
        out_shape=[jax.ShapeDtypeStruct(shape, kind) for shape, kind in finals],
        in_specs=[pl.BlockSpec(memory_space=smem)] + [whole((count, width))] * slices + [by_rows] * 3 + [whole(x.shape) for x in sums],
        out_specs=[by_rows] * 4 + [by_step(shape) for shape, _ in finals[4:14]] + [whole(shape) for shape, _ in finals[14:]],
        compiler_params=pltpu.CompilerParams(vmem_limit_bytes=VMEM_LIMIT),
    )(part.reshape(1, 1).astype(jnp.int32), *mixed_blocks, query_state_grad, content_grad, encoded_grad, *sums)
    (
        mixed, query_state_grad, content_grad, encoded_grad, w_query_grad, w_key_grad, w_value_grad, w_out_grad,
        w_cross_query_grad, w_cross_key_grad, w_cross_value_grad, w_cross_out_grad, w_inner_grad, w_outer_grad, *gains,
    ) = results
    gains = [g.reshape(width) for g in gains]
    return (
        mixed, query_state_grad, content_grad, encoded_grad, w_query_grad, w_key_grad, w_value_grad, w_out_grad, gains[0],
        w_cross_query_grad, w_cross_key_grad, w_cross_value_grad, w_cross_out_grad, gains[1], w_inner_grad, w_outer_grad, gains[2],
    )


def solution(mesh):
    rows, whole, columns, split = P("seq", None), P(), P(None, "head"), P("head", None)
    in_specs = (
        rows, rows, rows, whole, whole, whole, columns, columns, columns, split, whole,
        columns, columns, columns, split, whole, columns, split, whole, rows,
    )
    out_specs = (
        rows, rows, rows, rows, columns, columns, columns, split, whole,
        columns, columns, columns, split, whole, columns, split, whole,
    )
    return jax.shard_map(body, mesh=mesh, in_specs=in_specs, out_specs=out_specs, check_vma=False)
```

profile of v0, /device:TPU:0, one launch (start us, length us, event | category | flops | bytes accessed | tf_op | source)
XLA Modules:
  0.0 350.1 jit_solution(4985460414146025215)
XLA Ops:
  7.2 0.0 all-gather.2.cloned.1.call-start
  7.2 1.3 copy.37
  8.5 0.7 fusion
  9.2 0.0 all-gather.2.cloned.1.call-update
  9.3 0.0 reduce-scatter.2.cloned.1.call-start
  9.3 0.8 dynamic_slice.10
  10.1 0.6 reshape.73.cut
  10.7 1.4 fusion.1.score
  12.1 48.9 %shard_map.323 = (bf16[3072,512]{1,0:T(8,128)(2,1)}, bf16[3072,512]{1,0:T(8,128)(2,1)}, bf16[4,384,512]{2,1,0:T(8,128)(2,1)}, bf16[4,640,512]{2,1,0:T(8,128)(2,1...) custom-call(bf16[1536,512]{1,0:T(8,128)(2,1)} %content.1, ...), custom_call_target="tpu_custom_call" | custom-call | flops 80000000000 | bytes 80000000 | tf_op jit(solution)/shard_map/pallas_call | solution.py:1045
  61.0 16.2 %shard_map.324 = (f32[512,384]{1,0:T(8,128)}, f32[8,384]{1,0:T(8,128)}, f32[384,512]{1,0:T(8,128)}, f32[512,384]{1,0:T(8,128)}, f32[8,384]{1,0:T(8,128)}) custom-call(s32[1,6]{1,0:T(1,128)} %get-tuple-element.68.bounds, bf16[384,512]{1,0:T(8,128)(2,1)} %get-tuple-element.69.own, bf16[3072,512]{1,0:T(8,128)(2,1)} %get-tuple-element.70.content_window.window_in, ...), custom_call_target="tpu_custom_call" | custom-call | flops 20000000000 | bytes 20000000 | tf_op jit(solution)/shard_map/pallas_call | solution.py:1029
  77.1 4.2 %all-gather.2.cloned.1.call-done = bf16[4096,512]{1,0:T(8,128)(2,1)} async-done(((bf16[128,512]{1,0:T(8,128)(2,1)}), bf16[4096,512]{1,0:T(8,128)(2,1)}) %all-gather.2.cloned.1.call-update) | async-done | bytes 4194320 | tf_op jit(solution)/shard_map/all_gather | solution.py:1082
  81.3 13.0 %shard_map.325 = (bf16[384,512]{1,0:T(8,128)(2,1)}, f32[384,512]{1,0:T(8,128)}, bf16[512,512]{1,0:T(8,128)(2,1)}, bf16[8,4,128,512]{3,2,1,0:T(8,128)(2,1)}, f32[1,512]{1,0:T(1,128)}, /*index=5*/f32[1,512]{1,0:T(1,128)}) custom-call(f32[384,512]{1,0:T(8,128)} %get-tuple-element.78.hidden_one, f32[512,384]{1,0:T(8,128)} %get-tuple-element.79.cross_t, ...), custom_call_target="tpu_custom_call" | custom-call | flops 20000000000 | bytes 20000000 | tf_op jit(solution)/shard_map/pallas_call | solution.py:1029
  94.3 0.0 copy-start
  94.3 0.0 reduce-scatter.2.cloned.1.call-update
  94.4 1.0 copy-done
  95.3 3.3 collective-permute-start.2
  98.6 2.4 collective-permute-start.1
  101.1 2.0 collective-permute-start
  103.1 17.5 %shard_map.326 = (f32[384,512]{1,0:T(8,128)}, bf16[3072,512]{1,0:T(8,128)(2,1)}, bf16[4,768,512]{2,1,0:T(8,128)(2,1)}) custom-call(s32[1,6]{1,0:T(1,128)} %get-tuple-element.68.bounds, bf16[384,512]{1,0:T(8,128)(2,1)} %get-tuple-element.69.own, f32[512,384]{1,0:T(8,128)} %get-tuple-element.82.self_t, f32[1,512]{1,0:T(1,128)} %bitcast.19, ...), custom_call_target="tpu_custom_call" | custom-call | flops 4000000000 | bytes 4000000 | tf_op jit(solution)/shard_map/pallas_call | solution.py:1029
  120.6 15.3 %shard_map.327 = (bf16[384,512]{1,0:T(8,128)(2,1)}, bf16[3072,512]{1,0:T(8,128)(2,1)}, bf16[4,384,512]{2,1,0:T(8,128)(2,1)}) custom-call(s32[1,6]{1,0:T(1,128)} %get-tuple-element.68.bounds, bf16[384,512]{1,0:T(8,128)(2,1)} %get-tuple-element.69.own, f32[384,512]{1,0:T(8,128)} %get-tuple-element.88.resid_one_grad, ...), custom_call_target="tpu_custom_call" | custom-call | flops 4000000000 | bytes 4000000 | tf_op jit(solution)/shard_map/pallas_call | solution.py:1029
  135.9 34.4 %reduce-scatter.2.cloned.1.call-done = bf16[1,4,128,512]{3,2,1,0:T(8,128)(2,1)} async-done(((bf16[8,4,128,512]{3,2,1,0:T(8,128)(2,1)}), bf16[1,4,128,512]{3,2,1,0:T(8,128)(2,1)}) %reduce-scatter.2.cloned.1.call-update) | async-done | bytes 524304 | tf_op jit(solution)/shard_map/reduce_scatter | solution.py:1146
  170.2 162.4 %shard_map.328 = (bf16[1536,512]{1,0:T(8,128)(2,1)}, bf16[1536,512]{1,0:T(8,128)(2,1)}, bf16[1536,512]{1,0:T(8,128)(2,1)}, bf16[384,512]{1,0:T(8,128)(2,1)}, bf1...) custom-call(bf16[384,512]{1,0:T(8,128)(2,1)} %get-tuple-element.90.refs_0_, ...), custom_call_target="tpu_custom_call" | custom-call | flops 80000000000 | bytes 80000000 | tf_op jit(solution)/shard_map/pallas_call | solution.py:1045
  332.6 0.0 collective-permute-done.2.refs_3_
  332.6 0.0 copy-start.1
  332.6 0.0 collective-permute-done.1.refs_2_
  332.6 0.0 copy-start.2
  332.6 0.0 collective-permute-done.refs_1_
  332.7 0.0 copy-start.3
  332.7 0.7 copy-done.1
  333.4 0.1 copy-done.2
  333.6 0.1 copy-done.3
  333.6 9.2 %shard_map.329 = (bf16[1536,512]{1,0:T(8,128)(2,1)}, f32[1536,512]{1,0:T(8,128)}, f32[1536,512]{1,0:T(8,128)}, f32[1536,512]{1,0:T(8,128)}, f32[512,128]{1,0:T(8...) custom-call(s32[1,1]{1,0:T(1,128)} %bitcast.part, ...), custom_call_target="tpu_custom_call" | custom-call | tf_op jit(solution)/shard_map/pallas_call | solution.py:1191
Async XLA Ops:
  7.2 74.1 %all-gather.2.cloned.1.call-start = ((), (), s32[]{:S(2)}) async-start(), calls=%async_computation.1 | async-start | bytes 4325376 | tf_op jit(solution)/shard_map/all_gather | solution.py:1082
  9.3 161.0 %reduce-scatter.2.cloned.1.call-start = ((), (), s32[]{:S(2)}) async-start(), calls=%async_computation.2 | async-start | bytes 4718592 | tf_op jit(solution)/shard_map/reduce_scatter | solution.py:1146
  94.3 1.0 copy-start
  95.3 237.3 %collective-permute-start.2 = (bf16[384,512]{1,0:T(8,128)(2,1)S(1)}, bf16[384,512]{1,0:T(8,128)(2,1)S(1)}, u32[]{:S(2)}, u32[]{:S(2)}) collective-permute-start(bf16[384,512]{1,0:T(8,128)(2,1)S(1)} %copy-done), channel_id=1, source_target_pairs={{0,3},{1,0},{2,1},{3,2},{4,7},{5,4},{6,5},{7,6},{8,11},{9,8},{10,9... | collective-permute-start | bytes 1179656 | tf_op jit(solution)/shard_map/ppermute | solution.py:1145
  98.6 234.0 %collective-permute-start.1 = (bf16[384,512]{1,0:T(8,128)(2,1)S(1)}, bf16[384,512]{1,0:T(8,128)(2,1)S(1)}, u32[]{:S(2)}, u32[]{:S(2)}) collective-permute-start(bf16[384,512]{1,0:T(8,128)(2,1)S(1)} %copy-done), channel_id=1, source_target_pairs={{0,2},{1,3},{2,0},{3,1},{4,6},{5,7},{6,4},{7,5},{8,10},{9,11},{10,... | collective-permute-start | bytes 1179656 | tf_op jit(solution)/shard_map/ppermute | solution.py:1145
  101.1 231.6 %collective-permute-start = (bf16[384,512]{1,0:T(8,128)(2,1)S(1)}, bf16[384,512]{1,0:T(8,128)(2,1)S(1)}, u32[]{:S(2)}, u32[]{:S(2)}) collective-permute-start(bf16[384,512]{1,0:T(8,128)(2,1)S(1)} %copy-done), channel_id=1, source_target_pairs={{0,1},{1,2},{2,3},{3,0},{4,5},{5,6},{6,7},{7,4},{8,9},{9,10},{10,1... | collective-permute-start | bytes 1179656 | tf_op jit(solution)/shard_map/ppermute | solution.py:1145
  332.6 0.8 copy-start.1
  332.6 0.9 copy-start.2
  332.7 1.0 copy-start.3
Sparse Core Ops, SparseCore 0:
  11.5 69.7 all-gather.1
  94.5 75.6 reduce-scatter.1
where the time goes:
time: 349 us; the launch traced here: 350 us
  Pallas kernels  282 us (81%)
  waiting for transfers between devices  38.6 us (11%)
  between operations  14.6 us (4%)
  starting transfers between devices  7.86 us (2%)
  local copies, waits for them, and re-layouts  5.93 us (2%)
    pallas_call x2, Pallas kernels, talk(): pl.pallas_call(kernel, out_shape=[jax.ShapeDtypeStruct(shape, kind) for s...  211 us
    pallas_call x4, Pallas kernels, call(): pl.pallas_call(kernel, out_shape=[jax.ShapeDtypeStruct(shape, kind) for s...  61.9 us
    reduce_scatter x1, waiting for transfers between devices, body(): lax.psum_scatter(grads_three, 'seq', scatter_dimension=0, tiled=True)  34.4 us
    pallas_call x1, Pallas kernels, body(): pl.pallas_call(partial(finish_kernel, cols, units, slices), grid=(slices,...  9.2 us
    ppermute x3, starting transfers between devices, body(): lax.ppermute(mixed, 'head', [(i, (i + d) % slices) for i in range(slices)])  7.78 us
  transfers between devices with their start and end apart: 5, of which 2 were waited for; matrix products, arithmetic and copies ran while one was open for 1% of the time, Pallas kernels for 74%

commit v1 on v0

--- a/solution.py
+++ b/solution.py
@@ -180,7 +180,11 @@
 
 
 def find_sentences(begin, count, total_rows, lengths, score, cut, code, low, high_self, high_cross, bounds, blocks_code):
-    blocks, lanes = score.shape
+    lanes, blocks = score.shape[1], code.shape[0] // score.shape[1]
+    first_block = (begin - DOC_LEN) // lanes
+    for j in range(blocks):
+        at = jnp.clip(first_block + j, 0, score.shape[0] - 1)
+        blocks_code[j : j + 1, :] = score[pl.ds(at, 1), :].astype(F32)
     pos = lax.broadcasted_iota(jnp.int32, (blocks, lanes), 0) * lanes + lax.broadcasted_iota(jnp.int32, (blocks, lanes), 1)
     pos = pos + (begin - DOC_LEN)
     own_pos = lax.broadcasted_iota(jnp.int32, (1, count), 1) + begin
@@ -205,15 +209,17 @@
     none = lengths[0, 0] * 0
     carry = (none, zero, zero, jnp.zeros((1, count), jnp.int32), none, none, (none,) * 4)
     _, sentence, first, own_sentence, first_row, last_row, thirds = lax.fori_loop(0, lengths.shape[1], one, carry)
-    shown = jnp.where(pos == first, -1, score[...])
+    shown = jnp.where(pos == first, -1.0, blocks_code[0:blocks, :])
     inside = jnp.logical_and(pos >= 0, pos < total_rows)
-    blocks_code[0:blocks, :] = jnp.where(inside, sentence * CODES + shown, -CODES).astype(F32)
+    blocks_code[0:blocks, :] = jnp.where(inside, (sentence * CODES).astype(F32) + shown, -float(CODES))
     for b in range(0, blocks, 8):
         turned = blocks_code[b : b + 8, :].T
         for j in range(min(8, blocks - b)):
             code[(b + j) * lanes : (b + j + 1) * lanes, :] = turned[:, j : j + 1]
     low[...] = (own_sentence * CODES - 1).astype(F32)
-    high_self[...] = (own_sentence * CODES + cut[...]).astype(F32)
+    for j in range(count // lanes):
+        some = slice(j * lanes, (j + 1) * lanes)
+        high_self[:, some] = (own_sentence[:, some] * CODES + cut[pl.ds(begin // lanes + j, 1), :]).astype(F32)
     high_cross[...] = (own_sentence * CODES + CODES // 2).astype(F32)
     origin = begin - DOC_LEN
     bounds[0, 0] = first_row - origin
@@ -718,12 +724,6 @@
     pack[:, index * size : (index + 1) * size, :] = value.astype(BF16).reshape(slices, size, value.shape[1])
 
 
-def write_pieces(pack, z, row, value):
-    size = pack.shape[2]
-    for i in range(value.shape[0] // size):
-        pack[row // size + i, z] = value[i * size : (i + 1) * size, :].astype(BF16)
-
-
 def mask_bias(code, low, high):
     return jnp.where((code >= low) & (code < high), 0.0, NEG_BIG).astype(F32)
 
@@ -848,7 +848,9 @@
     mixed, resid_grad, w_out_grad, grad_three_out, gain_cross_grad, gain_final_grad,
     normed_two, hidden_two_low, slope, active, sum_ffn, pack_out, pack_three, grad_three_pack, sems, out_sems,
 ):
-    slices, units = pack_three.shape[0], pack_three.shape[1] // 2
+    slices, units = pack_three.shape[0], active.shape[2]
+    if grad_three_pack.shape[1] > 2 * units:
+        grad_three_pack[:, 2 * units :, :] = jnp.zeros((slices, grad_three_pack.shape[1] - 2 * units, grad_three_pack.shape[2]), BF16)
     out_copy = pltpu.make_async_copy(pack_two.at[:, pl.ds(4 * cols, cols)], pack_out, sems.at[slices])
     out_copy.start()
     slice_copies = [pltpu.make_async_copy(pack_three_in.at[z], pack_three.at[z], sems.at[z]) for z in range(slices)]
@@ -868,18 +870,18 @@
         below = 0.5 * (1.0 + lax.erf(inner * math.sqrt(0.5)))
         slope[z] = below + inner * (jnp.exp2(inner * inner * (-0.5 * LOG2E)) * (1.0 / math.sqrt(2.0 * math.pi)))
         active[z] = (inner * below).astype(BF16)
-        sum_ffn[...] += dot_nn(active[z], pack_three[z, units:, :])
+        sum_ffn[...] += dot_nn(active[z], pack_three[z, units : 2 * units, :])
     normed_three, scale_three = layer_norm(sum_ffn[...])
     mixed[...] = (normed_three * gain_final[...]).astype(BF16)
     grad_three, gain_grad = norm_back(out_grad[...].astype(F32), normed_three, scale_three, gain_final[...])
     gain_final_grad[...] = gain_grad
     ffn_low = grad_three.astype(BF16)
-    result_copies = [pltpu.make_async_copy(grad_three_pack.at[:, z], grad_three_out.at[:, z], out_sems.at[z]) for z in range(slices)]
+    result_copies = [pltpu.make_async_copy(grad_three_pack.at[z], grad_three_out.at[z], out_sems.at[z]) for z in range(slices)]
     sum_ffn[...] = grad_three
     for z in range(slices):
-        write_pieces(grad_three_pack, z, units, dot_tn(active[z], ffn_low))
-        inner_low = (dot_nt(ffn_low, pack_three[z, units:, :]) * slope[z]).astype(BF16)
-        write_pieces(grad_three_pack, z, 0, dot_tn(inner_low, hidden_two_low[...]))
+        grad_three_pack[z, units : 2 * units, :] = dot_tn(active[z], ffn_low).astype(BF16)
+        inner_low = (dot_nt(ffn_low, pack_three[z, units : 2 * units, :]) * slope[z]).astype(BF16)
+        grad_three_pack[z, 0:units, :] = dot_tn(inner_low, hidden_two_low[...]).astype(BF16)
         sum_ffn[...] += dot_nn(inner_low, pack_three[z, 0:units, :])
         result_copies[z].start()
     grad, gain_grad = norm_back(sum_ffn[...], normed_two[...], scale_two, gain_cross[...])
@@ -984,19 +986,11 @@
     result.wait()
 
 
-def finish_kernel(cols, units, slices, part, *refs):
-    blocks, rows_in, (sum_one, sum_two, sum_three) = refs[:slices], refs[slices : slices + 3], refs[slices + 3 : slices + 6]
-    outs = refs[slices + 6 :]
+def finish_kernel(cols, units, slices, *refs):
+    rows_in, (sum_one, sum_two, sum_three), outs = refs[:4], refs[4:7], refs[7:]
     step = pl.program_id(0)
-    came = lax.rem(part[0, 0] + slices - step, slices)
-    for d, ref in enumerate(blocks):
-
-        @pl.when(came == d)
-        def _(ref=ref):
-            outs[0][...] = ref[...]
-
-    for source, target in zip(rows_in, outs[1:4]):
-        target[...] = source[...].astype(F32)
+    for source, target in zip(rows_in, outs[:4]):
+        target[...] = source[...].astype(target.dtype)
 
     def weights(k):
         w_query, w_key, w_value, w_out, w_cross_query, w_cross_key, w_cross_value, w_cross_out, w_inner, w_outer = outs[4:14]
@@ -1065,8 +1059,7 @@
     spare = wide - count - 2 * DOC_LEN
     seq, part = lax.axis_index("seq"), lax.axis_index("head")
     begin = seq * rows + part * count
-    score = lax.dynamic_slice_in_dim(jnp.pad(key_score, (DOC_LEN, DOC_LEN + spare)), begin, wide, 0).reshape(wide // lanes, lanes)
-    cut = lax.dynamic_slice_in_dim(query_cut, begin, count, 0).reshape(1, count)
+    score, cut = key_score.reshape(-1, lanes), query_cut.reshape(-1, lanes)
     gain_self, gain_cross, gain_final = (g.reshape(1, width) for g in (gain_self, gain_cross, gain_final))
 
     peers = lax.axis_size("seq")
@@ -1112,13 +1105,13 @@
     mixed, resid_two_grad, w_cross_out_grad, grads_three, gain_cross_grad, gain_final_grad = call(
         partial(ffn_kernel, cols),
         [
-            ((count, width), BF16), ((count, width), F32), ((width, width), BF16), ((peers, slices, grad_sizes[2] // peers, width), BF16),
+            ((count, width), BF16), ((count, width), F32), ((width, width), BF16), ((slices, grad_sizes[2], width), BF16),
             ((1, width), F32), ((1, width), F32),
         ],
         [
             ((count, width), F32), ((count, width), BF16), ((slices, count, units), F32),
             ((slices, count, units), BF16), ((count, width), F32), ((slices, cols, width), BF16), ((slices, sizes[2], width), BF16),
-            ((peers, slices, grad_sizes[2] // peers, width), BF16), (slices + 1, None), (slices, None),
+            ((slices, grad_sizes[2], width), BF16), (slices + 1, None), (slices, None),
         ], 0,
         hidden_one, cross_t, pack_two, gain_cross, pack_three, gain_final, own_out_grad, far=(2, 4), far_outs=(3,),
     )
@@ -1134,6 +1127,7 @@
         bounds, own, self_t, gain_self, resid_two_grad, cross_t, lse_cross, encoded_window, code, low, high_cross, pack_two,
         w_cross_out_grad, gain_cross_grad, gain_final_grad, far=(7,), far_outs=(1,), micros=4,
     )
+    mixed = lax.all_gather(mixed, "head", axis=0, tiled=True)
     own_grad, content_part, grads_one = call(
         partial(self_back_kernel, cols),
         [((count, width), BF16), ((wide, width), BF16), ((slices, grad_sizes[0], width), BF16)],
@@ -1142,9 +1136,7 @@
         far=(3, 6), far_outs=(1,), micros=4,
     )
 
-    mixed_blocks = [mixed] + [lax.ppermute(mixed, "head", [(i, (i + d) % slices) for i in range(slices)]) for d in range(1, slices)]
-    plane_three = lax.psum_scatter(grads_three, "seq", scatter_dimension=0, tiled=True).reshape(grads_three.shape[1:])
-    blocks, parts, grads, planes = [own_grad], [content_part, encoded_part], [grads_one, grads_two], [plane_three]
+    blocks, parts, grads, planes = [own_grad], [content_part, encoded_part], [grads_one, grads_two, grads_three], []
     weight_scratch = []
     for n in grad_sizes[: len(grads)]:
         half, size = n // 2, n // 2 // chips
@@ -1192,10 +1184,10 @@
         partial(finish_kernel, cols, units, slices),
         grid=(slices,),
         out_shape=[jax.ShapeDtypeStruct(shape, kind) for shape, kind in finals],
-        in_specs=[pl.BlockSpec(memory_space=smem)] + [whole((count, width))] * slices + [by_rows] * 3 + [whole(x.shape) for x in sums],
+        in_specs=[by_rows] * 4 + [whole(x.shape) for x in sums],
         out_specs=[by_rows] * 4 + [by_step(shape) for shape, _ in finals[4:14]] + [whole(shape) for shape, _ in finals[14:]],
         compiler_params=pltpu.CompilerParams(vmem_limit_bytes=VMEM_LIMIT),
-    )(part.reshape(1, 1).astype(jnp.int32), *mixed_blocks, query_state_grad, content_grad, encoded_grad, *sums)
+    )(mixed, query_state_grad, content_grad, encoded_grad, *sums)
     (
         mixed, query_state_grad, content_grad, encoded_grad, w_query_grad, w_key_grad, w_value_grad, w_out_grad,
         w_cross_query_grad, w_cross_key_grad, w_cross_value_grad, w_cross_out_grad, w_inner_grad, w_outer_grad, *gains,

time: 349 us -> 334 us (0.957); the launches traced: 350 us -> 329 us
  waiting for transfers between devices: 38.6 us -> 0.08 us
  Pallas kernels: 282 us -> 313 us
  starting transfers between devices: 7.86 us -> 0.08 us
  local copies, waits for them, and re-layouts: 5.93 us -> 1.25 us
    pallas_call x4, Pallas kernels: 61.9 us -> 98.2 us  [call(): pl.pallas_call(kernel, out_shape=[jax.ShapeDtypeStruct(shape, kind) for s...]
    reduce_scatter x1 -> x0, waiting for transfers between devices: 34.4 us -> none  [body(): lax.psum_scatter(grads_three, 'seq', scatter_dimension=0, tiled=True)]
    ppermute x3 -> x0, starting transfers between devices: 7.78 us -> none  [body(): lax.ppermute(mixed, 'head', [(i, (i + d) % slices) for i in range(slices)])]
    pallas_call x2, Pallas kernels: 211 us -> 205 us  [talk(): pl.pallas_call(kernel, out_shape=[jax.ShapeDtypeStruct(shape, kind) for s...]
    all_gather x1, waiting for transfers between devices: 4.15 us -> 0.02 us  [body(): lax.all_gather(share_three, ('head', 'seq'), axis=0, tiled=True)]
  transfers between devices with their start and end apart: 5 -> 2, of which waited for: 2 -> 0; matrix products, arithmetic and copies ran while one was open for 1% -> 0% of each run, Pallas kernels for 74% -> 88%
where the time goes in v1:
time: 334 us; the launch traced here: 329 us
  Pallas kernels  313 us (94%)
  between operations  14.6 us (4%)
    pallas_call x2, Pallas kernels, talk(): pl.pallas_call(kernel, out_shape=[jax.ShapeDtypeStruct(shape, kind) for s...  205 us
    pallas_call x4, Pallas kernels, call(): pl.pallas_call(kernel, out_shape=[jax.ShapeDtypeStruct(shape, kind) for s...  98.2 us
    pallas_call x1, Pallas kernels, body(): pl.pallas_call(partial(finish_kernel, cols, units, slices), grid=(slices,...  9.36 us
  transfers between devices with their start and end apart: 2, of which 0 were waited for; matrix products, arithmetic and copies ran while one was open for 0% of the time, Pallas kernels for 88%

profile of v1, /device:TPU:0, one launch (start us, length us, event | category | flops | bytes accessed | tf_op | source)
XLA Modules:
  0.0 329.3 jit_solution(15760564930227321629)
XLA Ops:
  7.2 0.0 all-gather.3.cloned.1.call-start
  7.2 1.3 copy.37
  8.5 0.7 fusion
  9.2 0.0 all-gather.3.cloned.1.call-update
  9.3 0.0 all-gather.5.cloned.1.call-start
  9.3 48.9 %shard_map.323 = (bf16[3072,512]{1,0:T(8,128)(2,1)}, bf16[3072,512]{1,0:T(8,128)(2,1)}, bf16[4,384,512]{2,1,0:T(8,128)(2,1)}, bf16[4,640,512]{2,1,0:T(8,128)(2,1...) custom-call(bf16[1536,512]{1,0:T(8,128)(2,1)} %content.1, ...), custom_call_target="tpu_custom_call" | custom-call | flops 80000000000 | bytes 80000000 | tf_op jit(solution)/shard_map/pallas_call | solution.py:1039
  58.2 26.9 %shard_map.324 = (f32[512,384]{1,0:T(8,128)}, f32[8,384]{1,0:T(8,128)}, f32[384,512]{1,0:T(8,128)}, f32[512,384]{1,0:T(8,128)}, f32[8,384]{1,0:T(8,128)}) custom-call(s32[1,6]{1,0:T(1,128)} %get-tuple-element.68.bounds, bf16[384,512]{1,0:T(8,128)(2,1)} %get-tuple-element.69.own, bf16[3072,512]{1,0:T(8,128)(2,1)} %get-tuple-element.70.content_window.window_in, ...), custom_call_target="tpu_custom_call" | custom-call | flops 20000000000 | bytes 20000000 | tf_op jit(solution)/shard_map/pallas_call | solution.py:1023
  85.1 0.0 all-gather.3.cloned.1.call-done
  85.1 13.0 %shard_map.325 = (bf16[384,512]{1,0:T(8,128)(2,1)}, f32[384,512]{1,0:T(8,128)}, bf16[512,512]{1,0:T(8,128)(2,1)}, bf16[4,1024,512]{2,1,0:T(8,128)(2,1)}, f32[1,512]{1,0:T(1,128)}, /*index=5*/f32[1,512]{1,0:T(1,128)}) custom-call(f32[384,512]{1,0:T(8,128)} %get-tuple-element.78.hidden_one, f32[512,384]{1,0:T(8,128)} %get-tuple-element.79.cross_t, ...), custom_call_target="tpu_custom_call" | custom-call | flops 20000000000 | bytes 20000000 | tf_op jit(solution)/shard_map/pallas_call | solution.py:1023
  98.2 0.0 all-gather.5.cloned.1.call-update
  98.2 29.6 %shard_map.326 = (f32[384,512]{1,0:T(8,128)}, bf16[3072,512]{1,0:T(8,128)(2,1)}, bf16[4,768,512]{2,1,0:T(8,128)(2,1)}) custom-call(s32[1,6]{1,0:T(1,128)} %get-tuple-element.68.bounds, bf16[384,512]{1,0:T(8,128)(2,1)} %get-tuple-element.69.own, f32[512,384]{1,0:T(8,128)} %get-tuple-element.82.self_t, f32[1,512]{1,0:T(1,128)} %bitcast.18, ...), custom_call_target="tpu_custom_call" | custom-call | flops 4000000000 | bytes 4000000 | tf_op jit(solution)/shard_map/pallas_call | solution.py:1023
  127.8 28.7 %shard_map.327 = (bf16[384,512]{1,0:T(8,128)(2,1)}, bf16[3072,512]{1,0:T(8,128)(2,1)}, bf16[4,384,512]{2,1,0:T(8,128)(2,1)}) custom-call(s32[1,6]{1,0:T(1,128)} %get-tuple-element.68.bounds, bf16[384,512]{1,0:T(8,128)(2,1)} %get-tuple-element.69.own, f32[384,512]{1,0:T(8,128)} %get-tuple-element.88.resid_one_grad, ...), custom_call_target="tpu_custom_call" | custom-call | flops 4000000000 | bytes 4000000 | tf_op jit(solution)/shard_map/pallas_call | solution.py:1023
  156.5 156.1 %shard_map.328 = (bf16[1536,512]{1,0:T(8,128)(2,1)}, bf16[1536,512]{1,0:T(8,128)(2,1)}, bf16[1536,512]{1,0:T(8,128)(2,1)}, bf16[384,512]{1,0:T(8,128)(2,1)}, bf1...) custom-call(bf16[384,512]{1,0:T(8,128)(2,1)} %get-tuple-element.90.refs_0_, ...), custom_call_target="tpu_custom_call" | custom-call | flops 80000000000 | bytes 80000000 | tf_op jit(solution)/shard_map/pallas_call | solution.py:1039
  312.6 0.0 all-gather.5.cloned.1.call-done.refs_0_
  312.7 9.4 %shard_map.329 = (bf16[1536,512]{1,0:T(8,128)(2,1)}, f32[1536,512]{1,0:T(8,128)}, f32[1536,512]{1,0:T(8,128)}, f32[1536,512]{1,0:T(8,128)}, f32[512,128]{1,0:T(8...) custom-call(bf16[1536,512]{1,0:T(8,128)(2,1)} %all-gather.5.cloned.1, ...), custom_call_target="tpu_custom_call" | custom-call | tf_op jit(solution)/shard_map/pallas_call | solution.py:1183
Async XLA Ops:
  7.2 77.9 %all-gather.3.cloned.1.call-start = ((), (), s32[]{:S(2)}) async-start(), calls=%async_computation | async-start | bytes 4325376 | tf_op jit(solution)/shard_map/all_gather | solution.py:1075
  9.3 303.4 %all-gather.5.cloned.1.call-start = ((), (), s32[]{:S(2)}) async-start(), calls=%async_computation.1 | async-start | bytes 1966080 | tf_op jit(solution)/shard_map/all_gather | solution.py:1130
Sparse Core Ops, SparseCore 0:
  11.5 69.7 all-gather.2
  98.3 47.1 all-gather.4
